TPU v7x, 32 devices: a whole 2x2x4 slice. The times are simulated.
32 devices in a mesh: sweep: 4 (over y, core), layer: 8 (over z, x).
Axes of the slice: x: 2, y: 2, z: 4, core: 2. Of those that a mesh axis runs over, the one named last changes fastest.
Arguments:
- face_rhs: float32 [4, 16, 32, 384], P('sweep', None, 'layer'), may hold values from -6 to 6
- res_rows: float32 [16384, 384], P(('sweep', 'layer')), may hold values from -4 to 4
- row_owner: int32 [16384, 1], P(('sweep', 'layer')), may hold values from 0 to 7; in each aligned block of 512 rows (0 to 511, 512 to 1023, ...) at most 128 rows name the same one
- row_slot: int32 [16384], P(('sweep', 'layer')), may hold values from 0 to 63
- inv_blocks: bfloat16 [4, 32, 384, 384], P('sweep', 'layer'), may hold values from -0.3125 to 0.3125
- couple_in: bfloat16 [4, 1536, 12288], P('sweep', None, 'layer'), may hold values from -0.15625 to 0.15625
- couple_out: bfloat16 [4, 12288, 1536], P('sweep', 'layer'), may hold values from -0.0546875 to 0.0546875
Outputs:
- solved: float32 [4, 16, 32, 384], P('sweep', None, 'layer')
Inputs may be any that keep to these rules, and one draw needn't show every extreme that they name: `row_owner`: among the 512 rows of one device no owner is named by more than 128 rows, a bound that some block reaches.
All inputs are finite; a program needn't handle non-finite values.
Results may differ from a plain program's by a relative error of at most 0.02.
Values may be sent and summed in bfloat16 or wider, within the bound.
A program may use at most 64 MiB of HBM per device.

v0:
```python
import jax
import jax.numpy as jnp
from jax import lax
from jax.sharding import PartitionSpec as P


def shifted(block, axis, distance):
    devices = range(lax.axis_size(axis))
    route = [(i - distance, i) for i in devices if i - distance in devices]
    return lax.ppermute(block, axis, route)


def on_device(face_rhs, res_rows, row_owner, row_slot, inv_blocks, couple_in, couple_out):
    group_size = lax.axis_size("layer")
    rhs_count = face_rhs.shape[1]
    face_dev = face_rhs.shape[2]
    face_width = face_rhs.shape[3]
    slot_count = rhs_count * face_dev
    row_total = res_rows.shape[0]
    owners = row_owner[:, 0]
    capacity = 2 * row_total // group_size
    matches = (owners[:, None] == jnp.arange(group_size, dtype=jnp.int32)[None, :]).astype(
        jnp.int32
    )
    earlier = jnp.cumsum(matches, axis=0) - matches
    position = jnp.sum(earlier * matches, axis=1)
    destination = owners * capacity + position
    send_rows = (
        jnp.zeros((group_size * capacity, face_width), jnp.float32).at[destination].set(res_rows)
    )
    send_slots = jnp.full((group_size * capacity,), -1, jnp.int32).at[destination].set(row_slot)
    got_rows, got_slots = (
        lax.all_to_all(
            send_rows.reshape(group_size, capacity, face_width),
            "layer",
            split_axis=0,
            concat_axis=0,
            tiled=True,
        ),
        lax.all_to_all(
            send_slots.reshape(group_size, capacity),
            "layer",
            split_axis=0,
            concat_axis=0,
            tiled=True,
        ),
    )
    one_hot = (jnp.arange(slot_count, dtype=jnp.int32)[:, None] == got_slots.reshape(1, -1)).astype(
        jnp.float32
    )
    added_rows = jnp.dot(one_hot, got_rows.reshape(-1, face_width), precision=lax.Precision.HIGHEST)
    assembled = face_rhs[0] + added_rows.reshape(rhs_count, face_dev, face_width)
    coupling_in = couple_in[0]
    coupling_out = couple_out[0]
    inverse = inv_blocks[0]

    def solve_layer(panel_in):
        coupled = jnp.dot(panel_in, coupling_in, preferred_element_type=jnp.float32)
        local_part = (assembled - coupled.reshape(rhs_count, face_dev, face_width)).astype(
            jnp.bfloat16
        )
        solved = jnp.einsum("rfw,fwv->rfv", local_part, inverse, preferred_element_type=jnp.float32)
        flattened = solved.astype(jnp.bfloat16).reshape(rhs_count, face_dev * face_width)
        panel_part = jnp.dot(flattened, coupling_out, preferred_element_type=jnp.float32)
        return (solved, panel_part)

    sections = lax.axis_size("sweep")
    own_index = lax.axis_index("sweep")
    panel_in = jnp.zeros((rhs_count, coupling_in.shape[0]), jnp.bfloat16)
    solved = jnp.zeros_like(assembled)
    panel_part = jnp.zeros((rhs_count, coupling_in.shape[0]), jnp.float32)
    for step_index in range(sections):
        solved, panel_part = lax.cond(
            own_index == step_index, lambda: solve_layer(panel_in), lambda: (solved, panel_part)
        )
        if step_index + 1 < sections:
            summed = lax.psum(panel_part, "layer").astype(jnp.bfloat16)
            arrived = shifted(summed, "sweep", 1)
            panel_in = arrived
    return solved[None]


def solution(mesh):
    return jax.shard_map(
        on_device,
        mesh=mesh,
        in_specs=(
            P("sweep", None, "layer", None),
            P(("sweep", "layer"), None),
            P(("sweep", "layer"), None),
            P(("sweep", "layer")),
            P("sweep", "layer", None, None),
            P("sweep", None, "layer"),
            P("sweep", "layer", None),
        ),
        out_specs=P("sweep", None, "layer", None),
        check_vma=False,
    )
```

profile of v0, /device:TPU:5, one launch (start us, length us, event | category | flops | bytes accessed | tf_op | source)
XLA Modules:
  0.0 191.7 jit_solution(7583375259851335154)
XLA Ops:
  0.0 0.8 fusion.28
  0.8 1.1 reduce-window.6
  2.2 0.8 fusion.27
  3.0 0.7 compare_select_fusion
  3.6 3.2 %scatter_custom_fusion = s32[1024]{0:T(1024)} fusion(s32[512]{0:T(512)S(1)} %bitcast.112, s32[512]{0:T(512)} %param.18, s32[]{:T(128)} %constant.10.clone.1), kind=kCustom, calls=%fused_computation.36 | custom fusion | bytes 4608 | tf_op jit(solution)/shard_map/scatter | solution.py:31
  6.8 5.5 %all-to-all-start = ((s32[8,1,128]{2,1,0:T(1,128)}), s32[8,1,128]{2,1,0:T(1,128)S(1)}, u32[]{:S(2)}, u32[]{:S(2)}) async-start(s32[8,1,128]{2,1,0:T(1,128)} %bitcast.15), calls=%async_computation | async-start | bytes 8192 | tf_op jit(solution)/shard_map/all_to_all | solution.py:40
  12.3 4.0 %scatter_custom_fusion.1 = f32[1024,384]{1,0:T(8,128)} fusion(s32[512]{0:T(512)S(1)} %bitcast.113, f32[512,384]{1,0:T(8,128)} %param.16, f32[]{:T(128)} %constant.32.clone.1), kind=kCustom, calls=%fused_computation.23 | custom fusion | bytes 1573376 | tf_op jit(solution)/shard_map/scatter | solution.py:29
  16.4 1.2 all-to-all-done
  17.6 4.2 %all-to-all-start.1 = ((f32[8,128,384]{2,1,0:T(8,128)}), f32[8,128,384]{2,1,0:T(8,128)S(1)}, u32[]{:S(2)}, u32[]{:S(2)}) async-start(f32[8,128,384]{2,1,0:T(8,128)} %bitcast.17), calls=%async_computation.1 | async-start | bytes 3145728 | tf_op jit(solution)/shard_map/all_to_all | solution.py:33
  21.8 35.6 %all-to-all-done.1 = f32[8,128,384]{2,1,0:T(8,128)S(1)} async-done(((f32[8,128,384]{2,1,0:T(8,128)}), f32[8,128,384]{2,1,0:T(8,128)S(1)}, u32[]{:S(2)}, u32[]{:S(2)}) %all-to-all-start.1) | async-done | bytes 1572896 | tf_op jit(solution)/shard_map/all_to_all | solution.py:33
  57.4 0.7 convolution_add_fusion
  58.1 0.7 conditional.4
  58.1 0.6 broadcast_in_dim.10
  58.8 30.9 %psum.21 = bf16[16,1536]{1,0:T(8,128)(2,1)S(1)} all-reduce(f32[16,1536]{1,0:T(8,128)S(1)} %get-tuple-element.81), channel_id=1, replica_groups=mesh['sweep'=4,'layer'=8] {'layer'}, use_global_device_ids=true, to_apply=%region_7.8 | all-reduce | flops 24576 | bytes 147456 | tf_op jit(solution)/shard_map/psum | solution.py:77
  89.6 1.3 collective-permute-start
  90.9 8.9 %collective-permute-done = bf16[16,1536]{1,0:T(8,128)(2,1)S(1)} collective-permute-done((bf16[16,1536]{1,0:T(8,128)(2,1)S(1)}, bf16[16,1536]{1,0:T(8,128)(2,1)S(1)}, u32[]{:S(2)}, u32[]{:S(2)}) %collective-permute-start) | collective-permute-done | bytes 49184 | tf_op jit(solution)/shard_map/ppermute | solution.py:10
  99.9 27.1 %psum.22 = bf16[16,1536]{1,0:T(8,128)(2,1)S(1)} all-reduce(f32[16,1536]{1,0:T(8,128)S(1)} %get-tuple-element.82), channel_id=1, replica_groups=mesh['sweep'=4,'layer'=8] {'layer'}, use_global_device_ids=true, to_apply=%region_10.11 | all-reduce | flops 24576 | bytes 147456 | tf_op jit(solution)/shard_map/psum | solution.py:77
  127.0 1.3 collective-permute-start.1
  128.3 10.8 %collective-permute-done.1 = bf16[16,1536]{1,0:T(8,128)(2,1)S(1)} collective-permute-done((bf16[16,1536]{1,0:T(8,128)(2,1)S(1)}, bf16[16,1536]{1,0:T(8,128)(2,1)S(1)}, u32[]{:S(2)}, u32[]{:S(2)}) %collective-permute-start.1) | collective-permute-done | bytes 49184 | tf_op jit(solution)/shard_map/ppermute | solution.py:10
  139.1 28.5 %psum.23 = bf16[16,1536]{1,0:T(8,128)(2,1)S(1)} all-reduce(f32[16,1536]{1,0:T(8,128)S(1)} %get-tuple-element.85), channel_id=1, replica_groups=mesh['sweep'=4,'layer'=8] {'layer'}, use_global_device_ids=true, to_apply=%region_13.14 | all-reduce | flops 24576 | bytes 147456 | tf_op jit(solution)/shard_map/psum | solution.py:77
  167.6 1.3 collective-permute-start.2
  168.9 18.7 %collective-permute-done.2 = bf16[16,1536]{1,0:T(8,128)(2,1)S(1)} collective-permute-done((bf16[16,1536]{1,0:T(8,128)(2,1)S(1)}, bf16[16,1536]{1,0:T(8,128)(2,1)S(1)}, u32[]{:S(2)}, u32[]{:S(2)}) %collective-permute-start.2) | collective-permute-done | bytes 49184 | tf_op jit(solution)/shard_map/ppermute | solution.py:10
  187.6 3.4 %conditional.7 = (f32[1,16,4,384]{3,2,1,0:T(4,128)S(1)}) conditional(s32[]{:T(128)} %convert_element_type.50, f32[16,4,384]{2,0,1:T(8,128)} %get-tuple-element.84, (bf16[16,1536]{1,0:T(8,128)(2,1)S(1)}, bf16[1536,1536]{1,0:T(8,128)(2,1)}, f32[16,4,384]{2,0,1:T(8,128)S(1)}, bf16[4,384,384]{2,1,0:T(8,128)(2,1)S(1)}) %tuple.70), branch_computations={%region_14.15_spmd, %region_15.16_spmd} | conditional | flops 94420992 | bytes 6537224 | solution.py:73
  187.6 3.1 %fusion.36 = f32[16,1536]{1,0:T(8,128)S(1)} fusion(bf16[16,1536]{1,0:T(8,128)(2,1)S(1)} %get-tuple-element.73, bf16[1536,1536]{1,0:T(8,128)(2,1)} %get-tuple-element.74), kind=kOutput, calls=%fused_computation.44 | convolution fusion | flops 75497472 | bytes 4866048 | tf_op jit(solution)/shard_map/cond/branch_1_fun/dot_general | solution.py:58
  (15 shorter events, 1.2 us)
Async XLA Ops:
  0.0 57.4 %copy-start.4 = (f32[1,16,4,384]{3,2,1,0:T(4,128)S(1)}, f32[1,16,4,384]{3,2,1,0:T(4,128)}, u32[]{:S(2)}) copy-start(f32[1,16,4,384]{3,2,1,0:T(4,128)} %param.15) | copy-start | bytes 294916
  0.0 58.1 %copy-start.2 = (bf16[1,4,384,384]{3,2,1,0:T(8,128)(2,1)S(1)}, bf16[1,4,384,384]{3,2,1,0:T(8,128)(2,1)}, u32[]{:S(2)}) copy-start(bf16[1,4,384,384]{3,2,1,0:T(8,128)(2,1)} %param.19) | copy-start | bytes 3538948
  6.8 10.8 %all-to-all-start = ((s32[8,1,128]{2,1,0:T(1,128)}), s32[8,1,128]{2,1,0:T(1,128)S(1)}, u32[]{:S(2)}, u32[]{:S(2)}) async-start(s32[8,1,128]{2,1,0:T(1,128)} %bitcast.15), calls=%async_computation | async-start | bytes 8192 | tf_op jit(solution)/shard_map/all_to_all | solution.py:40
  17.6 39.8 %all-to-all-start.1 = ((f32[8,128,384]{2,1,0:T(8,128)}), f32[8,128,384]{2,1,0:T(8,128)S(1)}, u32[]{:S(2)}, u32[]{:S(2)}) async-start(f32[8,128,384]{2,1,0:T(8,128)} %bitcast.17), calls=%async_computation.1 | async-start | bytes 3145728 | tf_op jit(solution)/shard_map/all_to_all | solution.py:33
  89.6 10.2 %collective-permute-start = (bf16[16,1536]{1,0:T(8,128)(2,1)S(1)}, bf16[16,1536]{1,0:T(8,128)(2,1)S(1)}, u32[]{:S(2)}, u32[]{:S(2)}) collective-permute-start(bf16[16,1536]{1,0:T(8,128)(2,1)S(1)} %psum.21), channel_id=1, source_target_pairs={{0,8},{8,16},{16,24},{1,9},{9,17},{17,25},{2,10},{10,18},{18,26},{... | collective-permute-start | bytes 147464 | tf_op jit(solution)/shard_map/ppermute | solution.py:10
  127.0 12.1 %collective-permute-start.1 = (bf16[16,1536]{1,0:T(8,128)(2,1)S(1)}, bf16[16,1536]{1,0:T(8,128)(2,1)S(1)}, u32[]{:S(2)}, u32[]{:S(2)}) collective-permute-start(bf16[16,1536]{1,0:T(8,128)(2,1)S(1)} %psum.22), channel_id=1, source_target_pairs={{0,8},{8,16},{16,24},{1,9},{9,17},{17,25},{2,10},{10,18},{18,26},{... | collective-permute-start | bytes 147464 | tf_op jit(solution)/shard_map/ppermute | solution.py:10
  167.6 20.0 %collective-permute-start.2 = (bf16[16,1536]{1,0:T(8,128)(2,1)S(1)}, bf16[16,1536]{1,0:T(8,128)(2,1)S(1)}, u32[]{:S(2)}, u32[]{:S(2)}) collective-permute-start(bf16[16,1536]{1,0:T(8,128)(2,1)S(1)} %psum.23), channel_id=1, source_target_pairs={{0,8},{8,16},{16,24},{1,9},{9,17},{17,25},{2,10},{10,18},{18,26},{... | collective-permute-start | bytes 147464 | tf_op jit(solution)/shard_map/ppermute | solution.py:10
  191.0 0.6 copy-start.3
where the time goes:
time: 192 us
  blocking collectives  86.5 us (45%)
  waiting for transfers between devices  75.2 us (39%)
  starting transfers between devices  13.6 us (7%)
  local copies, waits for them, and re-layouts  8.76 us (5%)
  matrix products  4.03 us (2%)
  other arithmetic  3.42 us (2%)
    psum x3, blocking collectives, on_device(): summed = lax.psum(panel_part, 'layer').astype(jnp.bfloat16)  86.5 us
    ppermute x3, waiting for transfers between devices, shifted(): return lax.ppermute(block, axis, route)  38.4 us
    all_to_all x1, waiting for transfers between devices, on_device(): lax.all_to_all(send_rows.reshape(group_size, capacity, face_width), 'laye...  35.6 us
    all_to_all x1, starting transfers between devices, on_device(): lax.all_to_all(send_slots.reshape(group_size, capacity), 'layer', split_a...  5.53 us
    all_to_all x1, starting transfers between devices, on_device(): lax.all_to_all(send_rows.reshape(group_size, capacity, face_width), 'laye...  4.23 us
    scatter x1, local copies, waits for them, and re-layouts, on_device(): jnp.zeros((group_size * capacity, face_width), jnp.float32).at[destination]  4.03 us
    ppermute x3, starting transfers between devices, shifted(): return lax.ppermute(block, axis, route)  3.88 us
  transfers between devices with their start and end apart: 5, of which 5 were waited for; matrix products, arithmetic and copies ran while one was open for 2% of the time, Pallas kernels for 0%

commit v1 on v0

v1 whole, which is shorter than its diff:
```python
import functools

import jax
import jax.numpy as jnp
from jax import lax
from jax.experimental import pallas as pl
from jax.experimental.pallas import tpu as pltpu
from jax.sharding import PartitionSpec as P

MESH = pl.DeviceIdType.MESH
F32 = jnp.float32
BF16 = jnp.bfloat16
SLICE = 256


def dot(a, b):
    return jnp.dot(a, b, preferred_element_type=F32)


def kernel(
    n, layers, deep_from,
    owner_ref, slot_ref, rows_ref, face_ref, inv_ref, cin_ref, cout_ref,
    out_ref,
    owner_v, slot_v, rows_v, face_v, inv_v, cin_v, cout_v, wide_v, deep_v,
    send_v, recv_v, part_sum_v, base_v, acc_v, pan_v, part_v, prec_v,
    load_sem, a_send, a_recv, r_send, r_recv, g_send, g_recv,
):
    s = lax.axis_index("sweep")
    i = lax.axis_index("layer")
    rhs, faces, w = face_v.shape
    slots = rhs * faces
    panel = cin_v.shape[0]
    own_w = faces * w
    pieces = panel // SLICE
    low = (n - pieces) // 2
    half = faces // 2
    half_rows = half * rhs
    half_w = half * w
    mine = i - low
    sums = (mine >= 0) & (mine < pieces)
    first, last = s == 0, s == layers - 1
    deep = (s >= deep_from) & (s < layers - 1)

    barrier = pltpu.get_barrier_semaphore()
    for k in range(1, n):
        pl.semaphore_signal(
            barrier, inc=1, device_id=(s, lax.rem(i + k, n)), device_id_type=MESH
        )

    @pl.when((s > 0) & sums)
    def _():
        for k in range(n):
            pl.semaphore_signal(
                barrier, inc=1, device_id=(s - 1, lax.rem(i + k, n)), device_id_type=MESH
            )

    def load(src, dst, index):
        return pltpu.make_async_copy(src, dst, load_sem.at[index])

    third = panel // 3
    load_owner = load(owner_ref, owner_v, 0)
    load_slot = load(slot_ref, slot_v, 1)
    load_rows = load(rows_ref, rows_v, 2)
    load_face = load(face_ref.at[0], face_v, 3)
    load_inv = load(inv_ref.at[0], inv_v, 4)
    load_out = load(cout_ref.at[0], cout_v, 5)
    load_in = [
        load(cin_ref.at[0, pl.ds(b * third, third)], cin_v.at[pl.ds(b * third, third)], 6 + b)
        for b in range(3)
    ]
    for copy in (load_owner, load_slot, load_rows, load_inv, load_face):
        copy.start()

    @pl.when(jnp.logical_not(first))
    def _():
        for copy in load_in:
            copy.start()

    load_out.start()

    load_owner.wait()
    load_slot.wait()
    slot = slot_v[...]
    target = owner_v[...] * slots + (slot % faces) * rhs + slot // faces
    load_rows.wait()
    rows = rows_v[...].astype(BF16)
    group = 4
    for g in range(0, n, group):
        place = lax.broadcasted_iota(jnp.int32, (group * slots, rows.shape[0]), 0) + g * slots
        hot = jnp.where(place == target, 1.0, 0.0).astype(BF16)
        summed = dot(hot, rows).astype(BF16)
        for j in range(group):
            send_v[g + j] = summed[j * slots : (j + 1) * slots]

    heard = (n - 1) + jnp.where(last, 0, pieces)
    pl.semaphore_wait(barrier, heard)

    def row_copy(k, q):
        to = lax.rem(i + k, n)
        part = pl.ds(q * half_rows, half_rows)
        return pltpu.make_async_remote_copy(
            src_ref=send_v.at[to, part],
            dst_ref=recv_v.at[i, part],
            send_sem=a_send.at[k, q],
            recv_sem=a_recv.at[i, q],
            device_id=(s, to),
            device_id_type=MESH,
        )

    def row_arrival(source, q):
        part = pl.ds(q * half_rows, half_rows)
        return pltpu.make_async_remote_copy(
            src_ref=send_v.at[source, part],
            dst_ref=recv_v.at[source, part],
            send_sem=a_send.at[0, q],
            recv_sem=a_recv.at[source, q],
            device_id=(s, source),
            device_id_type=MESH,
        )

    def send_rows():
        for q in range(2):
            for k in range(1, n):
                row_copy(k, q).start()

    def panel_copy(c):
        return pltpu.make_async_remote_copy(
            src_ref=part_v.at[c],
            dst_ref=prec_v.at[i],
            send_sem=r_send.at[c],
            recv_sem=r_recv.at[i],
            device_id=(s + 1, low + c),
            device_id_type=MESH,
        )

    def send_panel(c, value):
        part_v[c] = value.astype(BF16)
        panel_copy(c).start()

    def columns(c):
        return slice(c * SLICE, (c + 1) * SLICE)

    def assemble(q):
        for k in range(1, n):
            row_arrival(lax.rem(i + k, n), q).wait_recv()
        for f in range(q * half, (q + 1) * half):
            part = slice(f * rhs, (f + 1) * rhs)
            total = face_v[:, f, :] + send_v[i, part, :].astype(F32)
            for k in range(1, n):
                total = total + recv_v[lax.rem(i + k, n), part, :].astype(F32)
            local = total.astype(BF16)
            cols = slice(f * w, (f + 1) * w)
            acc_v[:, cols] = total
            base_v[:, cols] = dot(local, inv_v[f])

    @pl.when(jnp.logical_not(s == 1))
    def _():
        send_rows()

    load_inv.wait()
    load_face.wait()

    @pl.when(first)
    def _():
        load_out.wait()
        assemble(0)
        head = base_v[:, :half_w].astype(BF16)
        for c in range(pieces):
            part_sum_v[:, columns(c)] = dot(head, cout_v[:half_w, columns(c)])
        assemble(1)
        tail = base_v[:, half_w:].astype(BF16)
        for c in range(pieces):
            send_panel(c, part_sum_v[:, columns(c)] + dot(tail, cout_v[half_w:, columns(c)]))
        out_ref[...] = base_v[...]

    def wait_in():
        for copy in load_in:
            copy.wait()

    def arrive(c):
        @pl.when(mine != c)
        def _():
            pltpu.make_async_remote_copy(
                src_ref=pan_v.at[c],
                dst_ref=pan_v.at[c],
                send_sem=g_send.at[0],
                recv_sem=g_recv.at[c],
                device_id=(s, low + c),
                device_id_type=MESH,
            ).wait_recv()

    def spread_copy(k):
        return pltpu.make_async_remote_copy(
            src_ref=pan_v.at[mine],
            dst_ref=pan_v.at[mine],
            send_sem=g_send.at[k],
            recv_sem=g_recv.at[mine],
            device_id=(s, lax.rem(i + k, n)),
            device_id_type=MESH,
        )

    def sum_panel():
        @pl.when(sums)
        def _():
            total = None
            for j in range(n):
                pltpu.make_async_remote_copy(
                    src_ref=part_v.at[0],
                    dst_ref=prec_v.at[j],
                    send_sem=r_send.at[0],
                    recv_sem=r_recv.at[j],
                    device_id=(s, j),
                    device_id_type=MESH,
                ).wait_recv()
                value = prec_v[j].astype(F32)
                total = value if total is None else total + value
            pan_v[mine] = total.astype(BF16)
            for k in range(1, n):
                spread_copy(k).start()

    @pl.when(jnp.logical_not(first) & jnp.logical_not(deep))
    def _():
        for b in range(3):
            load_in[b].wait()
            part = slice(b * third, (b + 1) * third)
            for f in range(faces):
                cols = slice(f * w, (f + 1) * w)
                wide_v[part, cols] = dot(cin_v[part, cols], inv_v[f]).astype(BF16)

        @pl.when(s == 1)
        def _():
            send_rows()

        load_out.wait()
        assemble(0)
        assemble(1)
        sum_panel()
        for c in range(pieces):
            arrive(c)
            product = dot(pan_v[c], wide_v[columns(c), :])
            if c == 0:
                acc_v[...] = base_v[...] - product
            else:
                acc_v[...] = acc_v[...] - product
        solved = acc_v[...]
        out_ref[...] = solved

        @pl.when(jnp.logical_not(last))
        def _():
            flat = acc_v[...].astype(BF16)
            for c in range(pieces):
                send_panel(c, dot(flat, cout_v[:, columns(c)]))

    @pl.when(deep)
    def _():
        load_out.wait()

        @pl.loop(0, own_w // 512)
        def _(b):
            cols = pl.ds(pl.multiple_of(b * 512, 512), 512)
            for f in range(faces):
                part = slice(f * w, (f + 1) * w)
                wide_v[part, cols] = dot(inv_v[f], cout_v[part, cols]).astype(BF16)

        wait_in()

        @pl.loop(0, panel // SLICE)
        def _(b):
            cols = pl.ds(pl.multiple_of(b * SLICE, SLICE), SLICE)
            deep_v[:, cols] = dot(cin_v[...], wide_v[:, cols]).astype(BF16)

        assemble(0)
        assemble(1)
        kept = acc_v[...]
        out_ref[...] = kept
        flat = base_v[...].astype(BF16)
        for c in range(pieces):
            acc_v[:, columns(c)] = dot(flat, cout_v[:, columns(c)])
        sum_panel()
        for c in range(pieces - 1):
            arrive(c)
            acc_v[...] = acc_v[...] - dot(pan_v[c], deep_v[columns(c), :])
        arrive(pieces - 1)
        tail = pan_v[pieces - 1]
        for c in range(pieces):
            send_panel(c, acc_v[:, columns(c)] - dot(tail, deep_v[columns(pieces - 1), columns(c)]))
        for c in range(pieces):
            out_ref[...] = out_ref[...] - dot(pan_v[c], cin_v[columns(c), :])
        for f in range(faces):
            cols = slice(f * w, (f + 1) * w)
            out_ref[:, cols] = dot(out_ref[:, cols].astype(BF16), inv_v[f])

    for q in range(2):
        for k in range(1, n):
            row_copy(k, q).wait_send()

    @pl.when(jnp.logical_not(last))
    def _():
        for c in range(pieces):
            panel_copy(c).wait_send()

    @pl.when(jnp.logical_not(first) & sums)
    def _():
        for k in range(1, n):
            spread_copy(k).wait_send()


def on_device(
    n, layers, face_rhs, res_rows, row_owner, row_slot, inv_blocks, couple_in, couple_out
):
    _, rhs, faces, w = face_rhs.shape
    count = res_rows.shape[0]
    panel, own_w = couple_in.shape[1:]
    pieces = panel // SLICE
    any_ref = pl.BlockSpec(memory_space=pl.ANY)
    solved = pl.pallas_call(
        functools.partial(kernel, n, layers, 2),
        out_shape=jax.ShapeDtypeStruct((rhs, own_w), F32),
        in_specs=[any_ref] * 7,
        out_specs=pl.BlockSpec(memory_space=pltpu.VMEM),
        scratch_shapes=[
            pltpu.VMEM((1, count), jnp.int32),
            pltpu.VMEM((1, count), jnp.int32),
            pltpu.VMEM((count, w), F32),
            pltpu.VMEM((rhs, faces, w), F32),
            pltpu.VMEM((faces, w, w), BF16),
            pltpu.VMEM((panel, own_w), BF16),
            pltpu.VMEM((own_w, panel), BF16),
            pltpu.VMEM((panel, own_w), BF16),
            pltpu.VMEM((panel, panel), BF16),
            pltpu.VMEM((n, rhs * faces, w), BF16),
            pltpu.VMEM((n, rhs * faces, w), BF16),
            pltpu.VMEM((rhs, panel), F32),
            pltpu.VMEM((rhs, own_w), F32),
            pltpu.VMEM((rhs, panel), F32),
            pltpu.VMEM((pieces, rhs, SLICE), BF16),
            pltpu.VMEM((pieces, rhs, SLICE), BF16),
            pltpu.VMEM((n, rhs, SLICE), BF16),
            pltpu.SemaphoreType.DMA((9,)),
            pltpu.SemaphoreType.DMA((n, 2)),
            pltpu.SemaphoreType.DMA((n, 2)),
            pltpu.SemaphoreType.DMA((pieces,)),
            pltpu.SemaphoreType.DMA((n,)),
            pltpu.SemaphoreType.DMA((n,)),
            pltpu.SemaphoreType.DMA((pieces,)),
        ],
        compiler_params=pltpu.CompilerParams(
            collective_id=0, has_side_effects=True, vmem_limit_bytes=50 * 1024 * 1024
        ),
    )(
        row_owner.reshape(1, count),
        row_slot.reshape(1, count),
        res_rows,
        face_rhs,
        inv_blocks,
        couple_in,
        couple_out,
    )
    return solved.reshape(1, rhs, faces, w)


def solution(mesh):
    return jax.shard_map(
        functools.partial(on_device, mesh.shape["layer"], mesh.shape["sweep"]),
        mesh=mesh,
        in_specs=(
            P("sweep", None, "layer", None),
            P(("sweep", "layer"), None),
            P(("sweep", "layer"), None),
            P(("sweep", "layer")),
            P("sweep", "layer", None, None),
            P("sweep", None, "layer"),
            P("sweep", "layer", None),
        ),
        out_specs=P("sweep", None, "layer", None),
        check_vma=False,
    )
```

time: 192 us -> 45.8 us (0.24)
  blocking collectives: 86.5 us -> 0 us
  waiting for transfers between devices: 75.2 us -> 0 us
  Pallas kernels: 0 us -> 40.2 us
  starting transfers between devices: 13.6 us -> 0 us
  matrix products: 4.03 us -> 0 us
  local copies, waits for them, and re-layouts: 8.76 us -> 5.33 us
  other arithmetic: 3.42 us -> 0 us
    psum x3 -> x0, blocking collectives: 86.5 us -> none  [on_device(): summed = lax.psum(panel_part, 'layer').astype(jnp.bfloat16)]
    pallas_call x0 -> x1, Pallas kernels: none -> 40.2 us  [on_device(): pl.pallas_call(functools.partial(kernel, n, layers, 2), out_shape=jax.Sha...]
    ppermute x3 -> x0, waiting for transfers between devices: 38.4 us -> none  [shifted(): return lax.ppermute(block, axis, route)]
    all_to_all x2 -> x0, waiting for transfers between devices: 36.8 us -> none  [the longest x1 35.6 us: on_device(): lax.all_to_all(send_rows.reshape(group_size, capacity, face_width), 'laye...]
    all_to_all x2 -> x0, starting transfers between devices: 9.75 us -> none  [the longest x1 5.53 us: on_device(): lax.all_to_all(send_slots.reshape(group_size, capacity), 'layer', split_a...]
    scatter x2 -> x0, local copies, waits for them, and re-layouts: 7.19 us -> none  [the longest x1 4.03 us: on_device(): jnp.zeros((group_size * capacity, face_width), jnp.float32).at[destination]]
    dot_general x3 -> x0, matrix products: 4.03 us -> none  [the longest x1 3.05 us: solve_layer(): coupled = jnp.dot(panel_in, coupling_in, preferred_element_type=jnp.float32)]
    unnamed x6 -> x10, local copies, waits for them, and re-layouts: 0.64 us -> 4.66 us
  transfers between devices with their start and end apart: 5 -> 0, of which waited for: 5 -> 0; matrix products, arithmetic and copies ran while one was open for 2% -> 0% of each run, Pallas kernels for 0% -> 0%
where the time goes in v1:
time: 45.8 us; the launch traced here: 45.5 us
  Pallas kernels  40.2 us (88%)
  local copies, waits for them, and re-layouts  5.33 us (12%)
    pallas_call x1, Pallas kernels, on_device(): pl.pallas_call(functools.partial(kernel, n, layers, 2), out_shape=jax.Sha...  40.2 us
    unnamed x10, local copies, waits for them, and re-layouts  4.66 us

profile of v1, /device:TPU:5, one launch (start us, length us, event | category | flops | bytes accessed | tf_op | source)
XLA Modules:
  0.0 45.5 jit_solution(18309669902073746555)
XLA Ops:
  0.0 0.0 copy-start
  0.0 1.3 %copy-done = bf16[1,4,384,384]{3,2,1,0:T(8,128)(2,1)S(1)} copy-done((bf16[1,4,384,384]{3,2,1,0:T(8,128)(2,1)S(1)}, bf16[1,4,384,384]{3,2,1,0:T(8,128)(2,1)}, u32[]{:S(2)}) %copy-start) | copy-done | bytes 1179672
  1.3 0.0 copy-start.1
  1.3 1.1 %copy-done.1 = f32[512,384]{1,0:T(8,128)S(1)} copy-done((f32[512,384]{1,0:T(8,128)S(1)}, f32[512,384]{1,0:T(8,128)}, u32[]{:S(2)}) %copy-start.1) | copy-done | bytes 786456
  2.4 0.0 copy-start.2
  2.4 0.9 %copy-done.2 = f32[1,16,4,384]{3,2,1,0:T(4,128)S(1)} copy-done((f32[1,16,4,384]{3,2,1,0:T(4,128)S(1)}, f32[1,16,4,384]{3,2,1,0:T(4,128)}, u32[]{:S(2)}) %copy-start.2) | copy-done | bytes 98328
  3.3 0.0 copy-start.3
  3.3 0.7 %copy-done.3 = s32[512,1]{0,1:T(1,128)S(1)} copy-done((s32[512,1]{0,1:T(1,128)S(1)}, s32[512,1]{0,1:T(1,128)}, u32[]{:S(2)}) %copy-start.3) | copy-done | bytes 2072
  4.0 0.0 copy-start.4
  4.0 0.7 %copy-done.4 = s32[512]{0:T(512)S(1)} copy-done((s32[512]{0:T(512)S(1)}, s32[512]{0:T(512)}, u32[]{:S(2)}) %copy-start.4) | copy-done | bytes 2072
  4.7 40.2 %shard_map.73 = f32[16,1536]{1,0:T(8,128)S(1)} custom-call(s32[1,512]{1,0:T(1,128)S(1)} %bitcast.2, s32[1,512]{1,0:T(1,128)S(1)} %bitcast.3, f32[512,384]{1,0:T(8,128)S(1)} %copy-done.1, f32[1,16,4,384]{3,2,1,0:T(4,128)S(1)} %copy-done.2, bf16[1,4,384,384]{3,2,1,0:T(8,128)(2,1)S(1)} %copy-done, bf16[1,1536,1536]{2,1,0:T(8,128)(2,1)} %cin_ref.1, ...), custom_call_target="tpu_custom_call" | custom-call | tf_op jit(solution)/shard_map/pallas_call | solution.py:316
  44.8 0.7 %reshape.11 = f32[1,16,4,384]{3,2,1,0:T(4,128)} reshape(f32[16,1536]{1,0:T(8,128)S(1)} %shard_map.73) | data formatting | bytes 196608 | tf_op jit(solution)/shard_map/reshape | solution.py:359
Async XLA Ops:
  0.0 1.3 %copy-start = (bf16[1,4,384,384]{3,2,1,0:T(8,128)(2,1)S(1)}, bf16[1,4,384,384]{3,2,1,0:T(8,128)(2,1)}, u32[]{:S(2)}) copy-start(bf16[1,4,384,384]{3,2,1,0:T(8,128)(2,1)} %inv_ref.1) | copy-start | bytes 3538948
  1.3 1.1 %copy-start.1 = (f32[512,384]{1,0:T(8,128)S(1)}, f32[512,384]{1,0:T(8,128)}, u32[]{:S(2)}) copy-start(f32[512,384]{1,0:T(8,128)} %rows_ref.1) | copy-start | bytes 2359300
  2.4 0.9 %copy-start.2 = (f32[1,16,4,384]{3,2,1,0:T(4,128)S(1)}, f32[1,16,4,384]{3,2,1,0:T(4,128)}, u32[]{:S(2)}) copy-start(f32[1,16,4,384]{3,2,1,0:T(4,128)} %face_ref.1) | copy-start | bytes 294916
  3.3 0.7 %copy-start.3 = (s32[512,1]{0,1:T(1,128)S(1)}, s32[512,1]{0,1:T(1,128)}, u32[]{:S(2)}) copy-start(s32[512,1]{0,1:T(1,128)} %param.9) | copy-start | bytes 6148
  4.0 0.7 %copy-start.4 = (s32[512]{0:T(512)S(1)}, s32[512]{0:T(512)}, u32[]{:S(2)}) copy-start(s32[512]{0:T(512)} %param.10) | copy-start | bytes 6148

commit v2 on v1

--- a/solution.py
+++ b/solution.py
@@ -10,7 +10,7 @@
 MESH = pl.DeviceIdType.MESH
 F32 = jnp.float32
 BF16 = jnp.bfloat16
-SLICE = 256
+OWNERS = 4
 
 
 def dot(a, b):
@@ -31,8 +31,11 @@
     slots = rhs * faces
     panel = cin_v.shape[0]
     own_w = faces * w
-    pieces = panel // SLICE
+    pieces = OWNERS
+    width = panel // pieces
+    pair = 2 * width
     low = (n - pieces) // 2
+    near = jnp.where(i < n // 2, 0, 1)
     half = faces // 2
     half_rows = half * rhs
     half_w = half * w
@@ -40,19 +43,6 @@
     sums = (mine >= 0) & (mine < pieces)
     first, last = s == 0, s == layers - 1
     deep = (s >= deep_from) & (s < layers - 1)
-
-    barrier = pltpu.get_barrier_semaphore()
-    for k in range(1, n):
-        pl.semaphore_signal(
-            barrier, inc=1, device_id=(s, lax.rem(i + k, n)), device_id_type=MESH
-        )
-
-    @pl.when((s > 0) & sums)
-    def _():
-        for k in range(n):
-            pl.semaphore_signal(
-                barrier, inc=1, device_id=(s - 1, lax.rem(i + k, n)), device_id_type=MESH
-            )
 
     def load(src, dst, index):
         return pltpu.make_async_copy(src, dst, load_sem.at[index])
@@ -78,6 +68,19 @@
 
     load_out.start()
 
+    barrier = pltpu.get_barrier_semaphore()
+    for k in range(1, n):
+        pl.semaphore_signal(
+            barrier, inc=1, device_id=(s, lax.rem(i + k, n)), device_id_type=MESH
+        )
+
+    @pl.when((s > 0) & sums)
+    def _():
+        for k in range(n):
+            pl.semaphore_signal(
+                barrier, inc=1, device_id=(s - 1, lax.rem(i + k, n)), device_id_type=MESH
+            )
+
     load_owner.wait()
     load_slot.wait()
     slot = slot_v[...]
@@ -137,8 +140,12 @@
         part_v[c] = value.astype(BF16)
         panel_copy(c).start()
 
-    def columns(c):
-        return slice(c * SLICE, (c + 1) * SLICE)
+    def columns(h):
+        return slice(h * pair, (h + 1) * pair)
+
+    def send_pair(h, value):
+        for a in range(2):
+            send_panel(2 * h + a, value[:, a * width : (a + 1) * width])
 
     def assemble(q):
         for k in range(1, n):
@@ -165,12 +172,11 @@
         load_out.wait()
         assemble(0)
         head = base_v[:, :half_w].astype(BF16)
-        for c in range(pieces):
-            part_sum_v[:, columns(c)] = dot(head, cout_v[:half_w, columns(c)])
+        part_sum_v[...] = dot(head, cout_v[:half_w, :])
         assemble(1)
         tail = base_v[:, half_w:].astype(BF16)
-        for c in range(pieces):
-            send_panel(c, part_sum_v[:, columns(c)] + dot(tail, cout_v[half_w:, columns(c)]))
+        for h in range(2):
+            send_pair(h, part_sum_v[:, columns(h)] + dot(tail, cout_v[half_w:, columns(h)]))
         out_ref[...] = base_v[...]
 
     def wait_in():
@@ -188,6 +194,14 @@
                 device_id=(s, low + c),
                 device_id_type=MESH,
             ).wait_recv()
+
+    def arrived_pair(h):
+        for a in range(2):
+            arrive(2 * h + a)
+        return jnp.concatenate([pan_v[2 * h], pan_v[2 * h + 1]], axis=1)
+
+    def pair_rows(h):
+        return pl.ds(pl.multiple_of(h * pair, pair), pair)
 
     def spread_copy(k):
         return pltpu.make_async_remote_copy(
@@ -227,29 +241,20 @@
                 cols = slice(f * w, (f + 1) * w)
                 wide_v[part, cols] = dot(cin_v[part, cols], inv_v[f]).astype(BF16)
 
-        @pl.when(s == 1)
-        def _():
-            send_rows()
-
         load_out.wait()
         assemble(0)
         assemble(1)
         sum_panel()
-        for c in range(pieces):
-            arrive(c)
-            product = dot(pan_v[c], wide_v[columns(c), :])
-            if c == 0:
-                acc_v[...] = base_v[...] - product
-            else:
-                acc_v[...] = acc_v[...] - product
-        solved = acc_v[...]
+        acc_v[...] = base_v[...] - dot(arrived_pair(near), wide_v[pair_rows(near), :])
+        far = 1 - near
+        solved = acc_v[...] - dot(arrived_pair(far), wide_v[pair_rows(far), :])
         out_ref[...] = solved
 
         @pl.when(jnp.logical_not(last))
         def _():
-            flat = acc_v[...].astype(BF16)
-            for c in range(pieces):
-                send_panel(c, dot(flat, cout_v[:, columns(c)]))
+            flat = out_ref[...].astype(BF16)
+            for h in range(2):
+                send_pair(h, dot(flat, cout_v[:, columns(h)]))
 
     @pl.when(deep)
     def _():
@@ -262,11 +267,15 @@
                 part = slice(f * w, (f + 1) * w)
                 wide_v[part, cols] = dot(inv_v[f], cout_v[part, cols]).astype(BF16)
 
+        @pl.when(s == 1)
+        def _():
+            send_rows()
+
         wait_in()
 
-        @pl.loop(0, panel // SLICE)
+        @pl.loop(0, panel // 256)
         def _(b):
-            cols = pl.ds(pl.multiple_of(b * SLICE, SLICE), SLICE)
+            cols = pl.ds(pl.multiple_of(b * 256, 256), 256)
             deep_v[:, cols] = dot(cin_v[...], wide_v[:, cols]).astype(BF16)
 
         assemble(0)
@@ -274,18 +283,15 @@
         kept = acc_v[...]
         out_ref[...] = kept
         flat = base_v[...].astype(BF16)
-        for c in range(pieces):
-            acc_v[:, columns(c)] = dot(flat, cout_v[:, columns(c)])
+        acc_v[...] = dot(flat, cout_v[...])
         sum_panel()
-        for c in range(pieces - 1):
-            arrive(c)
-            acc_v[...] = acc_v[...] - dot(pan_v[c], deep_v[columns(c), :])
-        arrive(pieces - 1)
-        tail = pan_v[pieces - 1]
-        for c in range(pieces):
-            send_panel(c, acc_v[:, columns(c)] - dot(tail, deep_v[columns(pieces - 1), columns(c)]))
-        for c in range(pieces):
-            out_ref[...] = out_ref[...] - dot(pan_v[c], cin_v[columns(c), :])
+        acc_v[...] = acc_v[...] - dot(arrived_pair(near), deep_v[pair_rows(near), :])
+        far = 1 - near
+        rest = arrived_pair(far)
+        for h in range(2):
+            send_pair(h, acc_v[:, columns(h)] - dot(rest, deep_v[pair_rows(far), columns(h)]))
+        whole = jnp.concatenate([pan_v[c] for c in range(pieces)], axis=1)
+        out_ref[...] = out_ref[...] - dot(whole, cin_v[...])
         for f in range(faces):
             cols = slice(f * w, (f + 1) * w)
             out_ref[:, cols] = dot(out_ref[:, cols].astype(BF16), inv_v[f])
@@ -311,10 +317,10 @@
     _, rhs, faces, w = face_rhs.shape
     count = res_rows.shape[0]
     panel, own_w = couple_in.shape[1:]
-    pieces = panel // SLICE
-    any_ref = pl.BlockSpec(memory_space=pl.ANY)
+    pieces, width = OWNERS, panel // OWNERS
+    any_ref = pl.BlockSpec(memory_space=pltpu.HBM)
     solved = pl.pallas_call(
-        functools.partial(kernel, n, layers, 2),
+        functools.partial(kernel, n, layers, 1),
         out_shape=jax.ShapeDtypeStruct((rhs, own_w), F32),
         in_specs=[any_ref] * 7,
         out_specs=pl.BlockSpec(memory_space=pltpu.VMEM),
@@ -333,9 +339,9 @@
             pltpu.VMEM((rhs, panel), F32),
             pltpu.VMEM((rhs, own_w), F32),
             pltpu.VMEM((rhs, panel), F32),
-            pltpu.VMEM((pieces, rhs, SLICE), BF16),
-            pltpu.VMEM((pieces, rhs, SLICE), BF16),
-            pltpu.VMEM((n, rhs, SLICE), BF16),
+            pltpu.VMEM((pieces, rhs, width), BF16),
+            pltpu.VMEM((pieces, rhs, width), BF16),
+            pltpu.VMEM((n, rhs, width), BF16),
             pltpu.SemaphoreType.DMA((9,)),
             pltpu.SemaphoreType.DMA((n, 2)),
             pltpu.SemaphoreType.DMA((n, 2)),
@@ -345,7 +351,7 @@
             pltpu.SemaphoreType.DMA((pieces,)),
         ],
         compiler_params=pltpu.CompilerParams(
-            collective_id=0, has_side_effects=True, vmem_limit_bytes=50 * 1024 * 1024
+            collective_id=0, has_side_effects=True, vmem_limit_bytes=63 * 1024 * 1024
         ),
     )(
         row_owner.reshape(1, count),

time: 45.8 us -> 38.6 us (0.84)
  local copies, waits for them, and re-layouts: 5.33 us -> 1.57 us
  Pallas kernels: 40.2 us -> 36.9 us
    unnamed x10 -> x0, local copies, waits for them, and re-layouts: 4.66 us -> none
    pallas_call x1, Pallas kernels: 40.2 us -> 36.9 us  [on_device(): pl.pallas_call(functools.partial(kernel, n, layers, 1), out_shape=jax.Sha...]
    reshape x1, local copies, waits for them, and re-layouts: 0.67 us -> 1.57 us  [on_device(): return solved.reshape(1, rhs, faces, w)]
where the time goes in v2:
time: 38.6 us; the launch traced here: 38.5 us
  Pallas kernels  36.9 us (96%)
  local copies, waits for them, and re-layouts  1.57 us (4%)
    pallas_call x1, Pallas kernels, on_device(): pl.pallas_call(functools.partial(kernel, n, layers, 1), out_shape=jax.Sha...  36.9 us
    reshape x1, local copies, waits for them, and re-layouts, on_device(): return solved.reshape(1, rhs, faces, w)  1.57 us

profile of v2, /device:TPU:5, one launch (start us, length us, event | category | flops | bytes accessed | tf_op | source)
XLA Modules:
  0.0 38.5 jit_solution(893799637858533774)
XLA Ops:
  0.0 36.9 %shard_map.73 = f32[16,1536]{1,0:T(8,128)} custom-call(s32[1,512]{1,0:T(1,128)} %bitcast.2, s32[1,512]{1,0:T(1,128)} %bitcast.3, f32[512,384]{1,0:T(8,128)} %rows_ref.1, f32[1,16,4,384]{3,2,1,0:T(4,128)} %face_ref.1, bf16[1,4,384,384]{3,2,1,0:T(8,128)(2,1)} %inv_ref.1, bf16[1,1536,1536]{2,1,0:T(8,128)(2,1)} %cin_ref.1, bf16[1,1536,1536]{2,1,0:T(8,128)(2,1)} %cout_ref.1), custom_call_target="tpu_custom_call" | custom-call | tf_op jit(solution)/shard_map/pallas_call | solution.py:322
  36.9 1.6 %reshape.11 = f32[1,16,4,384]{3,2,1,0:T(4,128)} reshape(f32[16,1536]{1,0:T(8,128)} %shard_map.73) | data formatting | bytes 196608 | tf_op jit(solution)/shard_map/reshape | solution.py:365

commit v3 on v2

--- a/solution.py
+++ b/solution.py
@@ -18,11 +18,11 @@
 
 
 def kernel(
-    n, layers, deep_from,
+    n, layers,
     owner_ref, slot_ref, rows_ref, face_ref, inv_ref, cin_ref, cout_ref,
     out_ref,
     owner_v, slot_v, rows_v, face_v, inv_v, cin_v, cout_v, wide_v, deep_v,
-    send_v, recv_v, part_sum_v, base_v, acc_v, pan_v, part_v, prec_v,
+    send_v, recv_v, full_v, local_v, acc_v, out_v, pan_v, part_v, prec_v,
     load_sem, a_send, a_recv, r_send, r_recv, g_send, g_recv,
 ):
     s = lax.axis_index("sweep")
@@ -35,14 +35,12 @@
     width = panel // pieces
     pair = 2 * width
     low = (n - pieces) // 2
-    near = jnp.where(i < n // 2, 0, 1)
     half = faces // 2
     half_rows = half * rhs
     half_w = half * w
     mine = i - low
     sums = (mine >= 0) & (mine < pieces)
     first, last = s == 0, s == layers - 1
-    deep = (s >= deep_from) & (s < layers - 1)
 
     def load(src, dst, index):
         return pltpu.make_async_copy(src, dst, load_sem.at[index])
@@ -58,15 +56,8 @@
         load(cin_ref.at[0, pl.ds(b * third, third)], cin_v.at[pl.ds(b * third, third)], 6 + b)
         for b in range(3)
     ]
-    for copy in (load_owner, load_slot, load_rows, load_inv, load_face):
+    for copy in (load_owner, load_slot, load_rows):
         copy.start()
-
-    @pl.when(jnp.logical_not(first))
-    def _():
-        for copy in load_in:
-            copy.start()
-
-    load_out.start()
 
     barrier = pltpu.get_barrier_semaphore()
     for k in range(1, n):
@@ -86,6 +77,24 @@
     slot = slot_v[...]
     target = owner_v[...] * slots + (slot % faces) * rhs + slot // faces
     load_rows.wait()
+    load_inv.start()
+
+    @pl.when(last)
+    def _():
+        for copy in load_in:
+            copy.start()
+
+    @pl.when(jnp.logical_not(last))
+    def _():
+        load_out.start()
+
+    load_face.start()
+
+    @pl.when(jnp.logical_not(first | last))
+    def _():
+        for copy in load_in:
+            copy.start()
+
     rows = rows_v[...].astype(BF16)
     group = 4
     for g in range(0, n, group):
@@ -157,8 +166,8 @@
                 total = total + recv_v[lax.rem(i + k, n), part, :].astype(F32)
             local = total.astype(BF16)
             cols = slice(f * w, (f + 1) * w)
-            acc_v[:, cols] = total
-            base_v[:, cols] = dot(local, inv_v[f])
+            full_v[:, cols] = total
+            local_v[:, cols] = local
 
     @pl.when(jnp.logical_not(s == 1))
     def _():
@@ -166,18 +175,6 @@
 
     load_inv.wait()
     load_face.wait()
-
-    @pl.when(first)
-    def _():
-        load_out.wait()
-        assemble(0)
-        head = base_v[:, :half_w].astype(BF16)
-        part_sum_v[...] = dot(head, cout_v[:half_w, :])
-        assemble(1)
-        tail = base_v[:, half_w:].astype(BF16)
-        for h in range(2):
-            send_pair(h, part_sum_v[:, columns(h)] + dot(tail, cout_v[half_w:, columns(h)]))
-        out_ref[...] = base_v[...]
 
     def wait_in():
         for copy in load_in:
@@ -199,9 +196,6 @@
         for a in range(2):
             arrive(2 * h + a)
         return jnp.concatenate([pan_v[2 * h], pan_v[2 * h + 1]], axis=1)
-
-    def pair_rows(h):
-        return pl.ds(pl.multiple_of(h * pair, pair), pair)
 
     def spread_copy(k):
         return pltpu.make_async_remote_copy(
@@ -232,69 +226,75 @@
             for k in range(1, n):
                 spread_copy(k).start()
 
-    @pl.when(jnp.logical_not(first) & jnp.logical_not(deep))
+    def face(f):
+        return slice(f * w, (f + 1) * w)
+
+    @pl.when(last)
     def _():
         for b in range(3):
             load_in[b].wait()
             part = slice(b * third, (b + 1) * third)
             for f in range(faces):
-                cols = slice(f * w, (f + 1) * w)
-                wide_v[part, cols] = dot(cin_v[part, cols], inv_v[f]).astype(BF16)
-
-        load_out.wait()
+                wide_v[part, face(f)] = dot(cin_v[part, face(f)], inv_v[f]).astype(BF16)
         assemble(0)
         assemble(1)
+        for f in range(faces):
+            full_v[:, face(f)] = dot(local_v[:, face(f)], inv_v[f])
         sum_panel()
-        acc_v[...] = base_v[...] - dot(arrived_pair(near), wide_v[pair_rows(near), :])
-        far = 1 - near
-        solved = acc_v[...] - dot(arrived_pair(far), wide_v[pair_rows(far), :])
-        out_ref[...] = solved
-
-        @pl.when(jnp.logical_not(last))
-        def _():
-            flat = out_ref[...].astype(BF16)
-            for h in range(2):
-                send_pair(h, dot(flat, cout_v[:, columns(h)]))
-
-    @pl.when(deep)
+        full_v[...] = full_v[...] - dot(arrived_pair(0), wide_v[:pair, :])
+        solved = full_v[...] - dot(arrived_pair(1), wide_v[pair:, :])
+        for f in range(faces):
+            out_v[:, f, :] = solved[:, face(f)]
+
+    @pl.when(jnp.logical_not(last))
     def _():
         load_out.wait()
 
-        @pl.loop(0, own_w // 512)
+        @pl.loop(0, panel // 512)
         def _(b):
             cols = pl.ds(pl.multiple_of(b * 512, 512), 512)
             for f in range(faces):
-                part = slice(f * w, (f + 1) * w)
-                wide_v[part, cols] = dot(inv_v[f], cout_v[part, cols]).astype(BF16)
-
-        @pl.when(s == 1)
-        def _():
-            send_rows()
-
-        wait_in()
-
-        @pl.loop(0, panel // 256)
-        def _(b):
-            cols = pl.ds(pl.multiple_of(b * 256, 256), 256)
-            deep_v[:, cols] = dot(cin_v[...], wide_v[:, cols]).astype(BF16)
+                wide_v[face(f), cols] = dot(inv_v[f], cout_v[face(f), cols]).astype(BF16)
+
+        @pl.when(jnp.logical_not(first))
+        def _():
+            wait_in()
+
+            @pl.loop(0, panel // 256)
+            def _(b):
+                @pl.when((b == 2) & (s == 1))
+                def _():
+                    send_rows()
+
+                cols = pl.ds(pl.multiple_of(b * 256, 256), 256)
+                deep_v[:, cols] = dot(cin_v[...], wide_v[:, cols]).astype(BF16)
 
         assemble(0)
+        acc_v[...] = dot(local_v[:, :half_w], wide_v[:half_w, :])
         assemble(1)
-        kept = acc_v[...]
-        out_ref[...] = kept
-        flat = base_v[...].astype(BF16)
-        acc_v[...] = dot(flat, cout_v[...])
-        sum_panel()
-        acc_v[...] = acc_v[...] - dot(arrived_pair(near), deep_v[pair_rows(near), :])
-        far = 1 - near
-        rest = arrived_pair(far)
-        for h in range(2):
-            send_pair(h, acc_v[:, columns(h)] - dot(rest, deep_v[pair_rows(far), columns(h)]))
-        whole = jnp.concatenate([pan_v[c] for c in range(pieces)], axis=1)
-        out_ref[...] = out_ref[...] - dot(whole, cin_v[...])
+        tail = local_v[:, half_w:]
+
+        @pl.when(first)
+        def _():
+            for h in range(2):
+                send_pair(h, acc_v[:, columns(h)] + dot(tail, wide_v[half_w:, columns(h)]))
+
+        @pl.when(jnp.logical_not(first))
+        def _():
+            acc_v[...] = acc_v[...] + dot(tail, wide_v[half_w:, :])
+            sum_panel()
+            acc_v[...] = acc_v[...] - dot(arrived_pair(0), deep_v[:pair, :])
+            rest = arrived_pair(1)
+            for h in range(2):
+                send_pair(h, acc_v[:, columns(h)] - dot(rest, deep_v[pair:, columns(h)]))
+            whole = jnp.concatenate([pan_v[c] for c in range(pieces)], axis=1)
+            full_v[...] = full_v[...] - dot(whole, cin_v[...])
+
         for f in range(faces):
-            cols = slice(f * w, (f + 1) * w)
-            out_ref[:, cols] = dot(out_ref[:, cols].astype(BF16), inv_v[f])
+            out_v[:, f, :] = dot(full_v[:, face(f)].astype(BF16), inv_v[f])
+
+    store_out = pltpu.make_async_copy(out_v, out_ref.at[0], load_sem.at[9])
+    store_out.start()
 
     for q in range(2):
         for k in range(1, n):
@@ -309,6 +309,8 @@
     def _():
         for k in range(1, n):
             spread_copy(k).wait_send()
+
+    store_out.wait()
 
 
 def on_device(
@@ -319,11 +321,11 @@
     panel, own_w = couple_in.shape[1:]
     pieces, width = OWNERS, panel // OWNERS
     any_ref = pl.BlockSpec(memory_space=pltpu.HBM)
-    solved = pl.pallas_call(
-        functools.partial(kernel, n, layers, 1),
-        out_shape=jax.ShapeDtypeStruct((rhs, own_w), F32),
+    return pl.pallas_call(
+        functools.partial(kernel, n, layers),
+        out_shape=jax.ShapeDtypeStruct((1, rhs, faces, w), F32),
         in_specs=[any_ref] * 7,
-        out_specs=pl.BlockSpec(memory_space=pltpu.VMEM),
+        out_specs=any_ref,
         scratch_shapes=[
             pltpu.VMEM((1, count), jnp.int32),
             pltpu.VMEM((1, count), jnp.int32),
@@ -336,13 +338,14 @@
             pltpu.VMEM((panel, panel), BF16),
             pltpu.VMEM((n, rhs * faces, w), BF16),
             pltpu.VMEM((n, rhs * faces, w), BF16),
+            pltpu.VMEM((rhs, own_w), F32),
+            pltpu.VMEM((rhs, own_w), BF16),
             pltpu.VMEM((rhs, panel), F32),
-            pltpu.VMEM((rhs, own_w), F32),
-            pltpu.VMEM((rhs, panel), F32),
+            pltpu.VMEM((rhs, faces, w), F32),
             pltpu.VMEM((pieces, rhs, width), BF16),
             pltpu.VMEM((pieces, rhs, width), BF16),
             pltpu.VMEM((n, rhs, width), BF16),
-            pltpu.SemaphoreType.DMA((9,)),
+            pltpu.SemaphoreType.DMA((10,)),
             pltpu.SemaphoreType.DMA((n, 2)),
             pltpu.SemaphoreType.DMA((n, 2)),
             pltpu.SemaphoreType.DMA((pieces,)),
@@ -362,7 +365,6 @@
         couple_in,
         couple_out,
     )
-    return solved.reshape(1, rhs, faces, w)
 
 
 def solution(mesh):

time: 38.6 us -> 38.9 us (level)
    reshape x1 -> x0, local copies, waits for them, and re-layouts: 1.57 us -> none  [on_device(): return solved.reshape(1, rhs, faces, w)]
    unnamed x0 -> x1, local copies, waits for them, and re-layouts: none -> 1.54 us
where the time goes in v3:
time: 38.9 us; the launch traced here: 38.7 us
  Pallas kernels  37.1 us (95%)
  local copies, waits for them, and re-layouts  1.54 us (4%)
    pallas_call x1, Pallas kernels, on_device(): pl.pallas_call(functools.partial(kernel, n, layers), out_shape=jax.ShapeD...  37.1 us
    unnamed x1, local copies, waits for them, and re-layouts  1.54 us

profile of v3, /device:TPU:5, one launch (start us, length us, event | category | flops | bytes accessed | tf_op | source)
XLA Modules:
  0.0 38.7 jit_solution(5728459506911925860)
XLA Ops:
  0.0 37.1 %shard_map.73 = f32[1,16,4,384]{3,2,1,0:T(4,128)} custom-call(s32[1,512]{1,0:T(1,128)} %bitcast.2, s32[1,512]{1,0:T(1,128)} %bitcast.3, f32[512,384]{1,0:T(8,128)} %rows_ref.1, f32[1,16,4,384]{3,2,1,0:T(4,128)} %face_ref.1, bf16[1,4,384,384]{3,2,1,0:T(8,128)(2,1)} %inv_ref.1, bf16[1,1536,1536]{2,1,0:T(8,128)(2,1)} %cin_ref.1, bf16[1,1536,1536]{2,1,0:T(8,128)(2,1)} %cout_ref.1), custom_call_target="tpu_custom_call" | custom-call | tf_op jit(solution)/shard_map/pallas_call | solution.py:324
  37.2 1.5 %copy.9 = f32[1,16,4,384]{3,2,1,0:T(4,128)} copy(f32[1,16,4,384]{3,2,1,0:T(4,128)} %shard_map.73) | data formatting | bytes 196608

commit v4 on v3

--- a/solution.py
+++ b/solution.py
@@ -22,7 +22,7 @@
     owner_ref, slot_ref, rows_ref, face_ref, inv_ref, cin_ref, cout_ref,
     out_ref,
     owner_v, slot_v, rows_v, face_v, inv_v, cin_v, cout_v, wide_v, deep_v,
-    send_v, recv_v, full_v, local_v, acc_v, out_v, pan_v, part_v, prec_v,
+    send_v, recv_v, full_v, local_v, acc_v, pan_v, part_v, prec_v,
     load_sem, a_send, a_recv, r_send, r_recv, g_send, g_recv,
 ):
     s = lax.axis_index("sweep")
@@ -39,6 +39,7 @@
     half_rows = half * rhs
     half_w = half * w
     mine = i - low
+    others = sorted(range(1, n), key=lambda k: abs(k - n // 2))
     sums = (mine >= 0) & (mine < pieces)
     first, last = s == 0, s == layers - 1
 
@@ -132,7 +133,7 @@
 
     def send_rows():
         for q in range(2):
-            for k in range(1, n):
+            for k in others:
                 row_copy(k, q).start()
 
     def panel_copy(c):
@@ -223,7 +224,7 @@
                 value = prec_v[j].astype(F32)
                 total = value if total is None else total + value
             pan_v[mine] = total.astype(BF16)
-            for k in range(1, n):
+            for k in others:
                 spread_copy(k).start()
 
     def face(f):
@@ -244,7 +245,7 @@
         full_v[...] = full_v[...] - dot(arrived_pair(0), wide_v[:pair, :])
         solved = full_v[...] - dot(arrived_pair(1), wide_v[pair:, :])
         for f in range(faces):
-            out_v[:, f, :] = solved[:, face(f)]
+            out_ref[0, :, f, :] = solved[:, face(f)]
 
     @pl.when(jnp.logical_not(last))
     def _():
@@ -266,6 +267,10 @@
                 def _():
                     send_rows()
 
+                @pl.when((b == panel // 256 - 1) & (s == 1))
+                def _():
+                    sum_panel()
+
                 cols = pl.ds(pl.multiple_of(b * 256, 256), 256)
                 deep_v[:, cols] = dot(cin_v[...], wide_v[:, cols]).astype(BF16)
 
@@ -282,7 +287,11 @@
         @pl.when(jnp.logical_not(first))
         def _():
             acc_v[...] = acc_v[...] + dot(tail, wide_v[half_w:, :])
-            sum_panel()
+
+            @pl.when(s > 1)
+            def _():
+                sum_panel()
+
             acc_v[...] = acc_v[...] - dot(arrived_pair(0), deep_v[:pair, :])
             rest = arrived_pair(1)
             for h in range(2):
@@ -291,10 +300,7 @@
             full_v[...] = full_v[...] - dot(whole, cin_v[...])
 
         for f in range(faces):
-            out_v[:, f, :] = dot(full_v[:, face(f)].astype(BF16), inv_v[f])
-
-    store_out = pltpu.make_async_copy(out_v, out_ref.at[0], load_sem.at[9])
-    store_out.start()
+            out_ref[0, :, f, :] = dot(full_v[:, face(f)].astype(BF16), inv_v[f])
 
     for q in range(2):
         for k in range(1, n):
@@ -309,8 +315,6 @@
     def _():
         for k in range(1, n):
             spread_copy(k).wait_send()
-
-    store_out.wait()
 
 
 def on_device(
@@ -325,7 +329,7 @@
         functools.partial(kernel, n, layers),
         out_shape=jax.ShapeDtypeStruct((1, rhs, faces, w), F32),
         in_specs=[any_ref] * 7,
-        out_specs=any_ref,
+        out_specs=pl.BlockSpec(memory_space=pltpu.VMEM),
         scratch_shapes=[
             pltpu.VMEM((1, count), jnp.int32),
             pltpu.VMEM((1, count), jnp.int32),
@@ -341,11 +345,10 @@
             pltpu.VMEM((rhs, own_w), F32),
             pltpu.VMEM((rhs, own_w), BF16),
             pltpu.VMEM((rhs, panel), F32),
-            pltpu.VMEM((rhs, faces, w), F32),
             pltpu.VMEM((pieces, rhs, width), BF16),
             pltpu.VMEM((pieces, rhs, width), BF16),
             pltpu.VMEM((n, rhs, width), BF16),
-            pltpu.SemaphoreType.DMA((10,)),
+            pltpu.SemaphoreType.DMA((9,)),
             pltpu.SemaphoreType.DMA((n, 2)),
             pltpu.SemaphoreType.DMA((n, 2)),
             pltpu.SemaphoreType.DMA((pieces,)),
@@ -354,16 +357,21 @@
             pltpu.SemaphoreType.DMA((pieces,)),
         ],
         compiler_params=pltpu.CompilerParams(
-            collective_id=0, has_side_effects=True, vmem_limit_bytes=63 * 1024 * 1024
+            collective_id=0, has_side_effects=True, vmem_limit_bytes=50 * 1024 * 1024
         ),
     )(
-        row_owner.reshape(1, count),
-        row_slot.reshape(1, count),
-        res_rows,
-        face_rhs,
-        inv_blocks,
-        couple_in,
-        couple_out,
+        *(
+            pltpu.with_memory_space_constraint(operand, pltpu.HBM)
+            for operand in (
+                row_owner.reshape(1, count),
+                row_slot.reshape(1, count),
+                res_rows,
+                face_rhs,
+                inv_blocks,
+                couple_in,
+                couple_out,
+            )
+        )
     )
 
 

time: 38.9 us -> 35.5 us (0.913)
  Pallas kernels: 37.1 us -> 34.7 us
  local copies, waits for them, and re-layouts: 1.54 us -> 0.64 us
    pallas_call x1, Pallas kernels: 37.1 us -> 34.7 us  [on_device(): pl.pallas_call(functools.partial(kernel, n, layers), out_shape=jax.ShapeD...]
    unnamed x1, local copies, waits for them, and re-layouts: 1.54 us -> 0.64 us
where the time goes in v4:
time: 35.5 us; the launch traced here: 35.4 us
  Pallas kernels  34.7 us (98%)
  local copies, waits for them, and re-layouts  0.64 us (2%)
    pallas_call x1, Pallas kernels, on_device(): pl.pallas_call(functools.partial(kernel, n, layers), out_shape=jax.ShapeD...  34.7 us

profile of v4, /device:TPU:5, one launch (start us, length us, event | category | flops | bytes accessed | tf_op | source)
XLA Modules:
  0.0 35.4 jit_solution(3156678034041074432)
XLA Ops:
  0.0 34.7 %shard_map.73 = f32[1,16,4,384]{3,2,1,0:T(4,128)S(1)} custom-call(s32[1,512]{1,0:T(1,128)} %bitcast.2, s32[1,512]{1,0:T(1,128)} %bitcast.3, f32[512,384]{1,0:T(8,128)} %rows_ref.1, f32[1,16,4,384]{3,2,1,0:T(4,128)} %face_ref.1, bf16[1,4,384,384]{3,2,1,0:T(8,128)(2,1)} %inv_ref.1, bf16[1,1536,1536]{2,1,0:T(8,128)(2,1)} %cin_ref.1, bf16[1,1536,1536]{2,1,0:T(8,128)(2,1)} %cout_ref.1), custom_call_target="tpu_custom_call" | custom-call | tf_op jit(solution)/shard_map/pallas_call | solution.py:328
  34.7 0.6 %copy.9 = f32[1,16,4,384]{3,2,1,0:T(4,128)} copy(f32[1,16,4,384]{3,2,1,0:T(4,128)S(1)} %shard_map.73) | data formatting | bytes 196608

commit v5 on v4

--- a/solution.py
+++ b/solution.py
@@ -10,7 +10,7 @@
 MESH = pl.DeviceIdType.MESH
 F32 = jnp.float32
 BF16 = jnp.bfloat16
-OWNERS = 4
+TEAM = 4
 
 
 def dot(a, b):
@@ -28,19 +28,17 @@
     s = lax.axis_index("sweep")
     i = lax.axis_index("layer")
     rhs, faces, w = face_v.shape
-    slots = rhs * faces
     panel = cin_v.shape[0]
     own_w = faces * w
-    pieces = OWNERS
+    pieces = TEAM
+    teams = n // TEAM
     width = panel // pieces
-    pair = 2 * width
-    low = (n - pieces) // 2
+    pair = panel // 2
+    team, mine = i // TEAM, i % TEAM
     half = faces // 2
     half_rows = half * rhs
     half_w = half * w
-    mine = i - low
     others = sorted(range(1, n), key=lambda k: abs(k - n // 2))
-    sums = (mine >= 0) & (mine < pieces)
     first, last = s == 0, s == layers - 1
 
     def load(src, dst, index):
@@ -66,7 +64,7 @@
             barrier, inc=1, device_id=(s, lax.rem(i + k, n)), device_id_type=MESH
         )
 
-    @pl.when((s > 0) & sums)
+    @pl.when(s > 0)
     def _():
         for k in range(n):
             pl.semaphore_signal(
@@ -76,7 +74,13 @@
     load_owner.wait()
     load_slot.wait()
     slot = slot_v[...]
-    target = owner_v[...] * slots + (slot % faces) * rhs + slot // faces
+    slot_face = slot % faces
+    target = (
+        (slot_face // half) * (n * half_rows)
+        + owner_v[...] * half_rows
+        + (slot_face % half) * rhs
+        + slot // faces
+    )
     load_rows.wait()
     load_inv.start()
 
@@ -97,23 +101,23 @@
             copy.start()
 
     rows = rows_v[...].astype(BF16)
-    group = 4
-    for g in range(0, n, group):
-        place = lax.broadcasted_iota(jnp.int32, (group * slots, rows.shape[0]), 0) + g * slots
-        hot = jnp.where(place == target, 1.0, 0.0).astype(BF16)
-        summed = dot(hot, rows).astype(BF16)
-        for j in range(group):
-            send_v[g + j] = summed[j * slots : (j + 1) * slots]
-
-    heard = (n - 1) + jnp.where(last, 0, pieces)
-    pl.semaphore_wait(barrier, heard)
+    def sum_rows(q):
+        block = min(n, 8) * half_rows
+        for g in range(n * half_rows // block):
+            base = q * n * half_rows + g * block
+            place = lax.broadcasted_iota(jnp.int32, (block, rows.shape[0]), 0) + base
+            hot = jnp.where(place == target, 1.0, 0.0).astype(BF16)
+            summed = dot(hot, rows).astype(BF16)
+            for j in range(block // half_rows):
+                send_v[q, g * (block // half_rows) + j] = summed[
+                    j * half_rows : (j + 1) * half_rows
+                ]
 
     def row_copy(k, q):
         to = lax.rem(i + k, n)
-        part = pl.ds(q * half_rows, half_rows)
         return pltpu.make_async_remote_copy(
-            src_ref=send_v.at[to, part],
-            dst_ref=recv_v.at[i, part],
+            src_ref=send_v.at[q, to],
+            dst_ref=recv_v.at[q, i],
             send_sem=a_send.at[k, q],
             recv_sem=a_recv.at[i, q],
             device_id=(s, to),
@@ -121,58 +125,67 @@
         )
 
     def row_arrival(source, q):
-        part = pl.ds(q * half_rows, half_rows)
         return pltpu.make_async_remote_copy(
-            src_ref=send_v.at[source, part],
-            dst_ref=recv_v.at[source, part],
+            src_ref=send_v.at[q, source],
+            dst_ref=recv_v.at[q, source],
             send_sem=a_send.at[0, q],
             recv_sem=a_recv.at[source, q],
             device_id=(s, source),
             device_id_type=MESH,
         )
 
-    def send_rows():
-        for q in range(2):
-            for k in others:
-                row_copy(k, q).start()
-
-    def panel_copy(c):
+    def send_rows(q):
+        for k in others:
+            row_copy(k, q).start()
+
+    def panel_copy(c, m):
+        to = lax.rem(team + 1 + m, teams) * TEAM + c
         return pltpu.make_async_remote_copy(
             src_ref=part_v.at[c],
             dst_ref=prec_v.at[i],
-            send_sem=r_send.at[c],
+            send_sem=r_send.at[m, c],
             recv_sem=r_recv.at[i],
-            device_id=(s + 1, low + c),
+            device_id=(s + 1, to),
             device_id_type=MESH,
         )
-
-    def send_panel(c, value):
-        part_v[c] = value.astype(BF16)
-        panel_copy(c).start()
 
     def columns(h):
         return slice(h * pair, (h + 1) * pair)
 
     def send_pair(h, value):
-        for a in range(2):
-            send_panel(2 * h + a, value[:, a * width : (a + 1) * width])
+        per = pieces // 2
+        for a in range(per):
+            part_v[h * per + a] = value[:, a * width : (a + 1) * width].astype(BF16)
+        for m in range(teams):
+            for a in range(per):
+                panel_copy(h * per + a, m).start()
 
     def assemble(q):
         for k in range(1, n):
             row_arrival(lax.rem(i + k, n), q).wait_recv()
         for f in range(q * half, (q + 1) * half):
-            part = slice(f * rhs, (f + 1) * rhs)
-            total = face_v[:, f, :] + send_v[i, part, :].astype(F32)
+            part = slice((f - q * half) * rhs, (f - q * half + 1) * rhs)
+            total = face_v[:, f, :] + send_v[q, i, part, :].astype(F32)
             for k in range(1, n):
-                total = total + recv_v[lax.rem(i + k, n), part, :].astype(F32)
+                total = total + recv_v[q, lax.rem(i + k, n), part, :].astype(F32)
             local = total.astype(BF16)
             cols = slice(f * w, (f + 1) * w)
             full_v[:, cols] = total
             local_v[:, cols] = local
 
+    sum_rows(0)
+    heard = (n - 1) + jnp.where(last, 0, n)
+    pl.semaphore_wait(barrier, heard)
+
     @pl.when(jnp.logical_not(s == 1))
     def _():
-        send_rows()
+        send_rows(0)
+
+    sum_rows(1)
+
+    @pl.when(jnp.logical_not(s == 1))
+    def _():
+        send_rows(1)
 
     load_inv.wait()
     load_face.wait()
@@ -189,43 +202,43 @@
                 dst_ref=pan_v.at[c],
                 send_sem=g_send.at[0],
                 recv_sem=g_recv.at[c],
-                device_id=(s, low + c),
+                device_id=(s, team * TEAM + c),
                 device_id_type=MESH,
             ).wait_recv()
 
     def arrived_pair(h):
-        for a in range(2):
-            arrive(2 * h + a)
-        return jnp.concatenate([pan_v[2 * h], pan_v[2 * h + 1]], axis=1)
-
-    def spread_copy(k):
+        chunks = range(h * pieces // 2, (h + 1) * pieces // 2)
+        for c in chunks:
+            arrive(c)
+        return jnp.concatenate([pan_v[c] for c in chunks], axis=1)
+
+    def spread_copy(m):
         return pltpu.make_async_remote_copy(
             src_ref=pan_v.at[mine],
             dst_ref=pan_v.at[mine],
-            send_sem=g_send.at[k],
+            send_sem=g_send.at[m],
             recv_sem=g_recv.at[mine],
-            device_id=(s, lax.rem(i + k, n)),
+            device_id=(s, team * TEAM + lax.rem(mine + m, TEAM)),
             device_id_type=MESH,
         )
 
     def sum_panel():
-        @pl.when(sums)
-        def _():
-            total = None
-            for j in range(n):
-                pltpu.make_async_remote_copy(
-                    src_ref=part_v.at[0],
-                    dst_ref=prec_v.at[j],
-                    send_sem=r_send.at[0],
-                    recv_sem=r_recv.at[j],
-                    device_id=(s, j),
-                    device_id_type=MESH,
-                ).wait_recv()
-                value = prec_v[j].astype(F32)
-                total = value if total is None else total + value
-            pan_v[mine] = total.astype(BF16)
-            for k in others:
-                spread_copy(k).start()
+        total = None
+        for j in range(n):
+            pltpu.make_async_remote_copy(
+                src_ref=part_v.at[0],
+                dst_ref=prec_v.at[j],
+                send_sem=r_send.at[0, 0],
+                recv_sem=r_recv.at[j],
+                device_id=(s, j),
+                device_id_type=MESH,
+            ).wait_recv()
+        for j in range(n):
+            value = prec_v[j].astype(F32)
+            total = value if total is None else total + value
+        pan_v[mine] = total.astype(BF16)
+        for m in range(1, TEAM):
+            spread_copy(m).start()
 
     def face(f):
         return slice(f * w, (f + 1) * w)
@@ -265,7 +278,8 @@
             def _(b):
                 @pl.when((b == 2) & (s == 1))
                 def _():
-                    send_rows()
+                    send_rows(0)
+                    send_rows(1)
 
                 @pl.when((b == panel // 256 - 1) & (s == 1))
                 def _():
@@ -309,12 +323,13 @@
     @pl.when(jnp.logical_not(last))
     def _():
         for c in range(pieces):
-            panel_copy(c).wait_send()
-
-    @pl.when(jnp.logical_not(first) & sums)
-    def _():
-        for k in range(1, n):
-            spread_copy(k).wait_send()
+            for m in range(teams):
+                panel_copy(c, m).wait_send()
+
+    @pl.when(jnp.logical_not(first))
+    def _():
+        for m in range(1, TEAM):
+            spread_copy(m).wait_send()
 
 
 def on_device(
@@ -323,7 +338,7 @@
     _, rhs, faces, w = face_rhs.shape
     count = res_rows.shape[0]
     panel, own_w = couple_in.shape[1:]
-    pieces, width = OWNERS, panel // OWNERS
+    pieces, width = TEAM, panel // TEAM
     any_ref = pl.BlockSpec(memory_space=pltpu.HBM)
     return pl.pallas_call(
         functools.partial(kernel, n, layers),
@@ -340,8 +355,8 @@
             pltpu.VMEM((own_w, panel), BF16),
             pltpu.VMEM((panel, own_w), BF16),
             pltpu.VMEM((panel, panel), BF16),
-            pltpu.VMEM((n, rhs * faces, w), BF16),
-            pltpu.VMEM((n, rhs * faces, w), BF16),
+            pltpu.VMEM((2, n, rhs * faces // 2, w), BF16),
+            pltpu.VMEM((2, n, rhs * faces // 2, w), BF16),
             pltpu.VMEM((rhs, own_w), F32),
             pltpu.VMEM((rhs, own_w), BF16),
             pltpu.VMEM((rhs, panel), F32),
@@ -351,9 +366,9 @@
             pltpu.SemaphoreType.DMA((9,)),
             pltpu.SemaphoreType.DMA((n, 2)),
             pltpu.SemaphoreType.DMA((n, 2)),
-            pltpu.SemaphoreType.DMA((pieces,)),
+            pltpu.SemaphoreType.DMA((n // TEAM, pieces)),
             pltpu.SemaphoreType.DMA((n,)),
-            pltpu.SemaphoreType.DMA((n,)),
+            pltpu.SemaphoreType.DMA((TEAM,)),
             pltpu.SemaphoreType.DMA((pieces,)),
         ],
         compiler_params=pltpu.CompilerParams(

time: 35.5 us -> 35.8 us (level)
  no operation moved by 1% of the time
where the time goes in v5:
time: 35.8 us; the launch traced here: 35.7 us
  Pallas kernels  35 us (98%)
  local copies, waits for them, and re-layouts  0.64 us (2%)
    pallas_call x1, Pallas kernels, on_device(): pl.pallas_call(functools.partial(kernel, n, layers), out_shape=jax.ShapeD...  35 us

profile of v5, /device:TPU:5, one launch (start us, length us, event | category | flops | bytes accessed | tf_op | source)
XLA Modules:
  0.0 35.7 jit_solution(250191196257481163)
XLA Ops:
  0.0 35.0 %shard_map.73 = f32[1,16,4,384]{3,2,1,0:T(4,128)S(1)} custom-call(s32[1,512]{1,0:T(1,128)} %bitcast.2, s32[1,512]{1,0:T(1,128)} %bitcast.3, f32[512,384]{1,0:T(8,128)} %rows_ref.1, f32[1,16,4,384]{3,2,1,0:T(4,128)} %face_ref.1, bf16[1,4,384,384]{3,2,1,0:T(8,128)(2,1)} %inv_ref.1, bf16[1,1536,1536]{2,1,0:T(8,128)(2,1)} %cin_ref.1, bf16[1,1536,1536]{2,1,0:T(8,128)(2,1)} %cout_ref.1), custom_call_target="tpu_custom_call" | custom-call | tf_op jit(solution)/shard_map/pallas_call | solution.py:343
  35.0 0.6 %copy.9 = f32[1,16,4,384]{3,2,1,0:T(4,128)} copy(f32[1,16,4,384]{3,2,1,0:T(4,128)S(1)} %shard_map.73) | data formatting | bytes 196608

commit v6 on v5

--- a/solution.py
+++ b/solution.py
@@ -22,7 +22,7 @@
     owner_ref, slot_ref, rows_ref, face_ref, inv_ref, cin_ref, cout_ref,
     out_ref,
     owner_v, slot_v, rows_v, face_v, inv_v, cin_v, cout_v, wide_v, deep_v,
-    send_v, recv_v, full_v, local_v, acc_v, pan_v, part_v, prec_v,
+    send_v, recv_v, full_v, local_v, acc_v, pan_v, part_v, prec_v, sum_v,
     load_sem, a_send, a_recv, r_send, r_recv, g_send, g_recv,
 ):
     s = lax.axis_index("sweep")
@@ -66,9 +66,9 @@
 
     @pl.when(s > 0)
     def _():
-        for k in range(n):
+        for c in range(TEAM):
             pl.semaphore_signal(
-                barrier, inc=1, device_id=(s - 1, lax.rem(i + k, n)), device_id_type=MESH
+                barrier, inc=1, device_id=(s - 1, team * TEAM + c), device_id_type=MESH
             )
 
     load_owner.wait()
@@ -145,9 +145,22 @@
             dst_ref=prec_v.at[i],
             send_sem=r_send.at[m, c],
             recv_sem=r_recv.at[i],
-            device_id=(s + 1, to),
+            device_id=(s, to),
             device_id_type=MESH,
         )
+
+    def each_panel_copy(c, m, act):
+        def run():
+            copy = panel_copy(c, m)
+            copy.start() if act == "start" else copy.wait_send()
+
+        if m < teams - 1:
+            run()
+        else:
+
+            @pl.when(mine != c)
+            def _():
+                run()
 
     def columns(h):
         return slice(h * pair, (h + 1) * pair)
@@ -158,7 +171,7 @@
             part_v[h * per + a] = value[:, a * width : (a + 1) * width].astype(BF16)
         for m in range(teams):
             for a in range(per):
-                panel_copy(h * per + a, m).start()
+                each_panel_copy(h * per + a, m, "start")
 
     def assemble(q):
         for k in range(1, n):
@@ -174,7 +187,7 @@
             local_v[:, cols] = local
 
     sum_rows(0)
-    heard = (n - 1) + jnp.where(last, 0, n)
+    heard = (n - 1) + jnp.where(last, 0, TEAM)
     pl.semaphore_wait(barrier, heard)
 
     @pl.when(jnp.logical_not(s == 1))
@@ -195,16 +208,14 @@
             copy.wait()
 
     def arrive(c):
-        @pl.when(mine != c)
-        def _():
-            pltpu.make_async_remote_copy(
-                src_ref=pan_v.at[c],
-                dst_ref=pan_v.at[c],
-                send_sem=g_send.at[0],
-                recv_sem=g_recv.at[c],
-                device_id=(s, team * TEAM + c),
-                device_id_type=MESH,
-            ).wait_recv()
+        pltpu.make_async_remote_copy(
+            src_ref=pan_v.at[c],
+            dst_ref=pan_v.at[c],
+            send_sem=g_send.at[0],
+            recv_sem=g_recv.at[c],
+            device_id=(s, lax.rem(i + 1, n)),
+            device_id_type=MESH,
+        ).wait_recv()
 
     def arrived_pair(h):
         chunks = range(h * pieces // 2, (h + 1) * pieces // 2)
@@ -212,33 +223,35 @@
             arrive(c)
         return jnp.concatenate([pan_v[c] for c in chunks], axis=1)
 
-    def spread_copy(m):
+    def forward_copy(m):
         return pltpu.make_async_remote_copy(
-            src_ref=pan_v.at[mine],
+            src_ref=sum_v,
             dst_ref=pan_v.at[mine],
             send_sem=g_send.at[m],
             recv_sem=g_recv.at[mine],
-            device_id=(s, team * TEAM + lax.rem(mine + m, TEAM)),
+            device_id=(s + 1, team * TEAM + lax.rem(mine + m, TEAM)),
             device_id_type=MESH,
         )
 
-    def sum_panel():
-        total = None
-        for j in range(n):
+    forward_order = sorted(range(TEAM), key=lambda m: abs(m - TEAM // 2))
+
+    def forward_panel():
+        for k in range(1, n):
+            j = lax.rem(i + k, n)
             pltpu.make_async_remote_copy(
-                src_ref=part_v.at[0],
+                src_ref=sum_v,
                 dst_ref=prec_v.at[j],
                 send_sem=r_send.at[0, 0],
                 recv_sem=r_recv.at[j],
                 device_id=(s, j),
                 device_id_type=MESH,
             ).wait_recv()
-        for j in range(n):
-            value = prec_v[j].astype(F32)
-            total = value if total is None else total + value
-        pan_v[mine] = total.astype(BF16)
-        for m in range(1, TEAM):
-            spread_copy(m).start()
+        total = part_v[mine].astype(F32)
+        for k in range(1, n):
+            total = total + prec_v[lax.rem(i + k, n)].astype(F32)
+        sum_v[...] = total.astype(BF16)
+        for m in forward_order:
+            forward_copy(m).start()
 
     def face(f):
         return slice(f * w, (f + 1) * w)
@@ -254,7 +267,6 @@
         assemble(1)
         for f in range(faces):
             full_v[:, face(f)] = dot(local_v[:, face(f)], inv_v[f])
-        sum_panel()
         full_v[...] = full_v[...] - dot(arrived_pair(0), wide_v[:pair, :])
         solved = full_v[...] - dot(arrived_pair(1), wide_v[pair:, :])
         for f in range(faces):
@@ -281,10 +293,6 @@
                     send_rows(0)
                     send_rows(1)
 
-                @pl.when((b == panel // 256 - 1) & (s == 1))
-                def _():
-                    sum_panel()
-
                 cols = pl.ds(pl.multiple_of(b * 256, 256), 256)
                 deep_v[:, cols] = dot(cin_v[...], wide_v[:, cols]).astype(BF16)
 
@@ -297,19 +305,16 @@
         def _():
             for h in range(2):
                 send_pair(h, acc_v[:, columns(h)] + dot(tail, wide_v[half_w:, columns(h)]))
+            forward_panel()
 
         @pl.when(jnp.logical_not(first))
         def _():
             acc_v[...] = acc_v[...] + dot(tail, wide_v[half_w:, :])
-
-            @pl.when(s > 1)
-            def _():
-                sum_panel()
-
             acc_v[...] = acc_v[...] - dot(arrived_pair(0), deep_v[:pair, :])
             rest = arrived_pair(1)
             for h in range(2):
                 send_pair(h, acc_v[:, columns(h)] - dot(rest, deep_v[pair:, columns(h)]))
+            forward_panel()
             whole = jnp.concatenate([pan_v[c] for c in range(pieces)], axis=1)
             full_v[...] = full_v[...] - dot(whole, cin_v[...])
 
@@ -324,12 +329,9 @@
     def _():
         for c in range(pieces):
             for m in range(teams):
-                panel_copy(c, m).wait_send()
-
-    @pl.when(jnp.logical_not(first))
-    def _():
-        for m in range(1, TEAM):
-            spread_copy(m).wait_send()
+                each_panel_copy(c, m, "wait_send")
+        for m in range(TEAM):
+            forward_copy(m).wait_send()
 
 
 def on_device(
@@ -363,6 +365,7 @@
             pltpu.VMEM((pieces, rhs, width), BF16),
             pltpu.VMEM((pieces, rhs, width), BF16),
             pltpu.VMEM((n, rhs, width), BF16),
+            pltpu.VMEM((rhs, width), BF16),
             pltpu.SemaphoreType.DMA((9,)),
             pltpu.SemaphoreType.DMA((n, 2)),
             pltpu.SemaphoreType.DMA((n, 2)),

time: 35.8 us -> 36.8 us (1.028)
  Pallas kernels: 35 us -> 36 us
    pallas_call x1, Pallas kernels: 35 us -> 36 us  [on_device(): pl.pallas_call(functools.partial(kernel, n, layers), out_shape=jax.ShapeD...]
where the time goes in v6:
time: 36.8 us; the launch traced here: 36.7 us
  Pallas kernels  36 us (98%)
  local copies, waits for them, and re-layouts  0.64 us (2%)
    pallas_call x1, Pallas kernels, on_device(): pl.pallas_call(functools.partial(kernel, n, layers), out_shape=jax.ShapeD...  36 us

profile of v6, /device:TPU:5, one launch (start us, length us, event | category | flops | bytes accessed | tf_op | source)
XLA Modules:
  0.0 36.7 jit_solution(3219799165492896478)
XLA Ops:
  0.0 36.0 %shard_map.73 = f32[1,16,4,384]{3,2,1,0:T(4,128)S(1)} custom-call(s32[1,512]{1,0:T(1,128)} %bitcast.2, s32[1,512]{1,0:T(1,128)} %bitcast.3, f32[512,384]{1,0:T(8,128)} %rows_ref.1, f32[1,16,4,384]{3,2,1,0:T(4,128)} %face_ref.1, bf16[1,4,384,384]{3,2,1,0:T(8,128)(2,1)} %inv_ref.1, bf16[1,1536,1536]{2,1,0:T(8,128)(2,1)} %cin_ref.1, bf16[1,1536,1536]{2,1,0:T(8,128)(2,1)} %cout_ref.1), custom_call_target="tpu_custom_call" | custom-call | tf_op jit(solution)/shard_map/pallas_call | solution.py:345
  36.0 0.6 %copy.9 = f32[1,16,4,384]{3,2,1,0:T(4,128)} copy(f32[1,16,4,384]{3,2,1,0:T(4,128)S(1)} %shard_map.73) | data formatting | bytes 196608
